TPU v7x, 32 devices: a whole 2x2x4 slice. The times are simulated.
32 devices in a mesh: seq: 16 (over z, y, core), head: 2 (over x).
Axes of the slice: x: 2, y: 2, z: 4, core: 2. Of those that a mesh axis runs over, the one named last changes fastest.
Arguments:
- features: bfloat16 [16384, 1024], P('seq', 'head'), may hold values from -4.1875 to 4.1875
- cells: int32 [16384], P('seq'), may hold values from 0 to 16383, as said below
- conv7: bfloat16 [7, 7, 1024], P(None, None, 'head'), may hold values from -0.875 to 0.875
- conv5: bfloat16 [5, 5, 1024], P(None, None, 'head'), may hold values from -1.25 to 1.25
- conv3: bfloat16 [3, 3, 1024], P(None, None, 'head'), may hold values from -2 to 2
- conv_bias: bfloat16 [1024], P('head'), may hold values from -3 to 3
- w_qkv: bfloat16 [1024, 3, 1024], P(None, None, 'head'), may hold values from -5 to 5
Outputs:
- attended: bfloat16 [16384, 1024], P('seq', 'head')
Inputs may be any that keep to these rules, and one draw needn't show every extreme that they name: cells names each of the 16384 grid cells once. Of the 1024 entries held by one index of seq, at most 128 lie in any one band of 1024 consecutive cells, and exactly 128 lie in some band; every band receives exactly 128 from some index of seq.
All inputs are finite; a program needn't handle non-finite values.
Results may differ from a plain program's by a relative error of at most 0.0052.
Values may be sent and summed in bfloat16 or wider, within the bound.
A program may use at most 128 MiB of HBM per device.

v0:
```python
import math

import jax
import jax.numpy as jnp
from jax import lax
from jax.sharding import PartitionSpec as P

D = 1024
HEADS = 16
GRID_W = 256


def with_halo(shard, sides, width):
    for axis, dim in sides:
        count, length = (lax.axis_size(axis), shard.shape[dim])
        up = [(i, (i + 1) % count) for i in range(count - 1)]
        down = [(j, i) for i, j in up]
        last = lax.slice_in_dim(shard, length - width, length, axis=dim)
        first = lax.slice_in_dim(shard, 0, width, axis=dim)
        before = lax.ppermute(last, axis, up)
        after = lax.ppermute(first, axis, down)
        shard = jnp.concatenate([before, shard, after], axis=dim)
    return shard


def passed_along(block, axis, distance):
    devices = range(lax.axis_size(axis))
    route = [((i - distance) % len(devices), i) for i in devices]
    return lax.ppermute(block, axis, route)


def depthwise(padded, kernel, margin, height, width):
    reach = kernel.shape[0]
    result = jnp.zeros((height, width, padded.shape[2]), jnp.float32)
    for i in range(reach):
        for j in range(reach):
            result = (
                result
                + padded[margin + i : margin + i + height, margin + j : margin + j + width]
                * kernel[i, j]
            )
    return result


def mix(extended, band_rows, width, conv7, conv5, conv3, conv_bias):
    padded = jnp.pad(extended, ((0, 0), (3, 3), (0, 0))).astype(jnp.float32)
    mixed_sum = padded[3 : 3 + band_rows, 3 : 3 + width] + conv_bias.astype(jnp.float32)
    merged = conv7.astype(jnp.float32) + jnp.pad(
        conv5.astype(jnp.float32), ((1, 1), (1, 1), (0, 0))
    )
    merged = merged + jnp.pad(conv3.astype(jnp.float32), ((2, 2), (2, 2), (0, 0)))
    mixed_sum = mixed_sum + depthwise(padded, merged, 0, band_rows, width)
    return mixed_sum.astype(jnp.bfloat16).reshape(band_rows * width, extended.shape[2])


def attend_block(queries, own_keys, own_values, prior_keys, prior_values, score_scale):
    own_scores = (
        jnp.einsum("qhd,khd->qhk", queries, own_keys, preferred_element_type=jnp.float32)
        * score_scale
    )
    prior_scores = (
        jnp.einsum("qhd,khd->qhk", queries, prior_keys, preferred_element_type=jnp.float32)
        * score_scale
    )
    row_top = jnp.maximum(jnp.max(own_scores, axis=2), jnp.max(prior_scores, axis=2))[:, :, None]
    own_weight = jnp.exp(own_scores - row_top)
    prior_weight = jnp.exp(prior_scores - row_top)
    weight_sum = jnp.sum(own_weight, axis=2) + jnp.sum(prior_weight, axis=2)
    summed = jnp.einsum(
        "qhk,khd->qhd",
        own_weight.astype(jnp.bfloat16),
        own_values,
        preferred_element_type=jnp.float32,
    )
    summed = summed + jnp.einsum(
        "qhk,khd->qhd",
        prior_weight.astype(jnp.bfloat16),
        prior_values,
        preferred_element_type=jnp.float32,
    )
    return (summed / weight_sum[:, :, None]).astype(jnp.bfloat16)


def shards(features, cells, conv7, conv5, conv3, conv_bias, w_qkv):
    tok_dev, local_dim = features.shape
    members = lax.axis_size("seq")
    capacity = 2 * tok_dev // members
    owner_band = cells // tok_dev
    within = cells - owner_band * tok_dev
    onehot = (owner_band[:, None] == jnp.arange(members, dtype=jnp.int32)[None, :]).astype(
        jnp.int32
    )
    earlier = jnp.cumsum(onehot, axis=0) - onehot
    slot_index = owner_band * capacity + jnp.sum(earlier * onehot, axis=1)
    outgoing = jnp.zeros((members * capacity, local_dim), jnp.bfloat16).at[slot_index].set(features)
    targets = jnp.full((members * capacity,), tok_dev, jnp.int32).at[slot_index].set(within)
    arrived, places = (
        lax.all_to_all(outgoing, "seq", split_axis=0, concat_axis=0, tiled=True),
        lax.all_to_all(targets, "seq", split_axis=0, concat_axis=0, tiled=True),
    )
    band_grid = jnp.zeros((tok_dev + 1, local_dim), jnp.bfloat16).at[places].set(arrived)[:tok_dev]
    band_rows = tok_dev // GRID_W
    band_grid = band_grid.reshape(band_rows, GRID_W, local_dim)
    extended = with_halo(band_grid, (("seq", 0),), 3)
    ppeg = mix(extended, band_rows, GRID_W, conv7, conv5, conv3, conv_bias)
    weights = w_qkv.reshape(w_qkv.shape[0], 3 * local_dim)
    projected = jnp.dot(
        lax.all_gather(ppeg, "head", axis=1, tiled=True),
        weights,
        preferred_element_type=jnp.float32,
    ).astype(jnp.bfloat16)
    prior_keys, prior_values = passed_along(
        (projected[:, local_dim : 2 * local_dim], projected[:, 2 * local_dim :]), "seq", 1
    )
    head_dim = D // HEADS
    head_count = local_dim // head_dim
    score_scale = 1.0 / math.sqrt(head_dim)

    def to_heads(matrix):
        return matrix.reshape(tok_dev, head_count, head_dim)

    own_keys = to_heads(projected[:, local_dim : 2 * local_dim])
    own_values = to_heads(projected[:, 2 * local_dim :])
    prior_key_heads = to_heads(prior_keys)
    prior_value_heads = to_heads(prior_values)
    block_rows = min(512, tok_dev)
    query_blocks = projected[:, :local_dim].reshape(
        tok_dev // block_rows, block_rows, head_count, head_dim
    )
    attended = lax.map(
        lambda query_block: attend_block(
            query_block, own_keys, own_values, prior_key_heads, prior_value_heads, score_scale
        ),
        query_blocks,
    )
    return attended.reshape(tok_dev, local_dim)


def solution(mesh):
    placed = (
        P("seq", "head"),
        P("seq"),
        P(None, None, "head"),
        P(None, None, "head"),
        P(None, None, "head"),
        P("head"),
        P(None, None, "head"),
    )
    return jax.shard_map(
        shards, mesh=mesh, in_specs=placed, out_specs=P("seq", "head"), check_vma=False
    )
```

profile of v0, /device:TPU:0, one launch (start us, length us, event | category | flops | bytes accessed | tf_op | source)
XLA Modules:
  0.0 313.6 jit_solution(8628240258367330233)
XLA Ops:
  6.5 0.7 add_select_fusion
  7.2 4.5 %reduce-window.6 = s32[16,8,128]{2,1,0:T(8,128)S(1)} reduce-window(s32[16,8,128]{2,1,0:T(8,128)S(1)} %fusion.98, s32[]{:T(128)} %copy.53), window={size=1x1x128 pad=0_0x0_0x127_0}, to_apply=%region_0.1 | reduce-window | flops 2080768 | bytes 131076 | tf_op jit(solution)/shard_map/reduce-window
  11.8 0.1 slice.437
  11.8 0.1 copy.27
  12.0 0.1 copy.28
  12.1 0.1 broadcast_add_fusion
  12.2 0.7 multiply_subtract_fusion
  12.9 4.9 %scatter_custom_fusion = s32[2048]{0:T(1024)} fusion(s32[1024]{0:T(1024)S(1)} %get-tuple-element.139, s32[1024]{0:T(1024)S(1)} %get-tuple-element.138, s32[]{:T(128)} %constant.46.clone.1), kind=kCustom, calls=%fused_computation.160 | custom fusion | bytes 8196 | tf_op jit(solution)/shard_map/scatter | solution.py:96
  17.8 7.4 %all-to-all-start = ((s32[16,128,1]{1,2,0:T(1,128)}), s32[16,128,1]{1,2,0:T(1,128)S(1)}, u32[]{:S(2)}, u32[]{:S(2)}) async-start(s32[16,128,1]{1,2,0:T(1,128)} %bitcast.9), calls=%async_computation | async-start | bytes 16384 | tf_op jit(solution)/shard_map/all_to_all | solution.py:99
  25.2 7.2 %scatter_custom_fusion.1 = bf16[2048,512]{1,0:T(8,128)(2,1)} fusion(s32[1024]{0:T(1024)S(1)} %get-tuple-element.139, bf16[1024,512]{1,0:T(8,128)(2,1)} %param.9, bf16[]{:T(256)} %constant.45.clone.1), kind=kCustom, calls=%fused_computation.138 | custom fusion | bytes 2097664 | tf_op jit(solution)/shard_map/scatter | solution.py:95
  32.4 0.0 all-to-all-done
  32.4 6.0 %all-to-all-start.1 = ((bf16[16,128,512]{2,1,0:T(8,128)(2,1)}), bf16[16,128,512]{2,1,0:T(8,128)(2,1)S(1)}, u32[]{:S(2)}, u32[]{:S(2)}) async-start(bf16[16,128,512]{2,1,0:T(8,128)(2,1)} %bitcast.12), calls=%async_computation.1 | async-start | bytes 4194304 | tf_op jit(solution)/shard_map/all_to_all | solution.py:98
  38.4 0.0 all-gather.2.cloned.1.call-start
  38.4 41.0 %all-to-all-done.1 = bf16[16,128,512]{2,1,0:T(8,128)(2,1)S(1)} async-done(((bf16[16,128,512]{2,1,0:T(8,128)(2,1)}), bf16[16,128,512]{2,1,0:T(8,128)(2,1)S(1)}, u32[]{:S(2)}, u32[]{:S(2)}) %all-to-all-start.1) | async-done | bytes 2097184 | tf_op jit(solution)/shard_map/all_to_all | solution.py:98
  79.5 9.7 %scatter_custom_fusion.2 = bf16[1025,512]{1,0:T(8,128)(2,1)S(1)} fusion(s32[2048]{0:T(1024)S(1)} %bitcast.232, bf16[2048,512]{1,0:T(8,128)(2,1)S(1)} %bitcast.177, bf16[]{:T(256)} %constant.45.clone.1), kind=kCustom, calls=%fused_computation.140 | custom fusion | bytes 1049602 | tf_op jit(solution)/shard_map/scatter | solution.py:101
  89.2 0.1 fusion.105
  89.3 2.7 collective-permute-start
  92.1 1.5 collective-permute-start.1
  93.6 0.0 copy-done.3
  93.6 0.0 copy-done.4
  93.6 0.0 copy-done.5
  93.6 0.0 copy-done.6
  93.8 0.1 slice.440
  93.8 0.1 collective-permute-done
  93.9 4.5 %collective-permute-done.1 = bf16[3,256,512]{2,1,0:T(8,128)(2,1)S(1)} collective-permute-done((bf16[3,256,512]{2,1,0:T(8,128)(2,1)S(1)}, bf16[3,256,512]{2,1,0:T(8,128)(2,1)S(1)}, u32[]{:S(2)}, u32[]{:S(2)}) %collective-permute-start.1) | collective-permute-done | bytes 786464 | tf_op jit(solution)/shard_map/ppermute | solution.py:21
  98.4 2.8 fusion.40
  101.2 47.4 %fusion.43 = bf16[4,256,512]{2,1,0:T(8,128)(2,1)} fusion(f32[10,262,512]{2,1,0:T(8,128)} %fusion.40, f32[512]{0:T(512)S(1)} %bitcast.195, f32[512]{0:T(512)S(1)} %bitcast.196, f32[512]{0:T(512)S(1)} %bitcast.197, f32[512]{0:T(512)S(1)} %bitcast.198, f32[512]{0:T(512)S(1)} %bitcast.199, f32[512]{0:T(512)S(1)} %bitcast.200, f32[512]{0:T(512)S(1)} %bitcast.201, ...), kind=kLoop, calls=%fused_computation.43 | loop fusion | flops 52428800 | bytes 103911424 | tf_op jit(solution)/shard_map/convert_element_type | solution.py:53
  148.6 0.0 all-gather.2.cloned.1.call-update
  148.6 0.0 copy-done.1
  148.6 3.1 copy.30
  151.7 49.3 %all-gather.2.cloned.1.call-done = bf16[1024,1024]{1,0:T(8,128)(2,1)} async-done(((bf16[1024,512]{1,0:T(8,128)(2,1)}), bf16[1024,1024]{1,0:T(8,128)(2,1)}) %all-gather.2.cloned.1.call-update) | async-done | bytes 2097168 | tf_op jit(solution)/shard_map/all_gather | solution.py:108
  201.0 6.0 %convolution_convert_fusion = bf16[1024,1536]{1,0:T(8,128)(2,1)S(1)} fusion(bf16[1024,1024]{1,0:T(8,128)(2,1)} %all-gather.2.cloned.1.call-done, bf16[1024,1536]{0,1:T(8,128)(2,1)} %bitcast.176), kind=kOutput, calls=%fused_computation.33 | convolution fusion | flops 3222798336 | bytes 8388608 | tf_op jit(solution)/shard_map/dot_general | solution.py:107
  206.9 1.2 fusion.104
  208.2 0.0 collective-permute-start.2
  208.2 1.6 collective-permute-start.3
  209.8 0.5 copy.32
  210.3 2.3 copy.34
  212.6 2.1 reshape.124
  214.7 2.5 copy.36
  217.2 8.0 %collective-permute-done.2 = bf16[1024,512]{1,0:T(8,128)(2,1)} collective-permute-done((bf16[1024,512]{1,0:T(8,128)(2,1)S(1)}, bf16[1024,512]{1,0:T(8,128)(2,1)}, u32[]{:S(2)}, u32[]{:S(2)}) %collective-permute-start.2) | collective-permute-done | bytes 1048608 | tf_op jit(solution)/shard_map/ppermute | solution.py:29
  225.2 1.5 copy.33
  226.7 9.7 %collective-permute-done.3 = bf16[1024,512]{1,0:T(8,128)(2,1)} collective-permute-done((bf16[1024,512]{1,0:T(8,128)(2,1)}, bf16[1024,512]{1,0:T(8,128)(2,1)}, u32[]{:S(2)}, u32[]{:S(2)}) %collective-permute-start.3) | collective-permute-done | bytes 1048608 | tf_op jit(solution)/shard_map/ppermute | solution.py:29
  236.4 2.3 copy.35
  238.7 63.3 %while.10 = (s32[]{:T(128)}, bf16[2,512,8,64]{1,3,2,0:T(8,128)(2,1)}, bf16[2,512,8,64]{1,3,2,0:T(8,128)(2,1)S(1)}, bf16[1024,8,64]{0,2,1:T(8,128)(2,1)S(1)}, bf1...) while((s32[]{:T(128)}, ...), condition=%wide.region_11.12_spmd, body=%wide.region_6.11_spmd.sunk | while | flops 2215370752 | bytes 117146264 | solution.py:130
  238.7 8.1 %bitcast_reduce_fusion.5 = (f32[512,8]{0,1:T(8,128)S(1)}, f32[8,512,1024]{2,1,0:T(8,128)}) fusion(bf16[1024,8,64]{0,2,1:T(8,128)(2,1)S(1)} %get-tuple-element.216, bf16[2,512,8,64]{1,3,2,0:T(8,128)(2,1)S(1)} %get-tuple-element.215, s32[]{:T(128)} %get-tuple-element.205), kind=kOutput, calls=%fused_computation.7.clone.1 | convolution fusion | flops 545255424 | bytes 18366468 | tf_op jit(solution)/shard_map/while/body/eval_jaxpr/qhd,khd->qhk/dot_general | solution.py:58
  246.8 2.5 bitcast_reduce_fusion.4
  249.3 0.0 copy-start
  249.3 9.2 %fusion.131 = (f32[512,8]{0,1:T(8,128)S(1)}, f32[512,8]{0,1:T(8,128)S(1)}) fusion(f32[8,512,1024]{2,1,0:T(8,128)S(1)} %get-tuple-element.191, f32[512,8]{0,1:T(8,128)S(1)} %max.8, f32[8,512,1024]{2,1,0:T(8,128)} %get-tuple-element.194), kind=kLoop, calls=%fused_computation.11.clone.1 | loop fusion | flops 25157632 | bytes 33603584 | tf_op jit(solution)/shard_map/while/body/eval_jaxpr/reduce_sum | solution.py:68
  258.5 0.0 copy-done
  258.6 0.0 copy-start.2
  258.6 3.7 %fusion.130 = f32[8,512,64]{1,2,0:T(8,128)S(1)} fusion(bf16[1024,8,64]{0,2,1:T(8,128)(2,1)S(1)} %copy-done, f32[8,512,1024]{2,1,0:T(8,128)S(1)} %get-tuple-element.191, f32[512,8]{0,1:T(8,128)S(1)} %max.8), kind=kOutput, calls=%fused_computation.13.clone.1 | convolution fusion | flops 549453824 | bytes 18890752 | tf_op jit(solution)/shard_map/while/body/eval_jaxpr/qhk,khd->qhd/dot_general | solution.py:75
  262.2 0.0 copy-done.2
  262.2 8.1 %fusion.132 = bf16[2,512,8,64]{1,3,2,0:T(8,128)(2,1)} fusion(bf16[2,512,8,64]{1,3,2,0:T(8,128)(2,1)} %get-tuple-element.206, s32[]{:T(128)} %get-tuple-element.205, f32[8,512,64]{1,2,0:T(8,128)S(1)} %fusion.130, bf16[1024,8,64]{0,2,1:T(8,128)(2,1)S(1)} %copy-done.2, f32[8,512,1024]{2,1,0:T(8,128)} %get-tuple-element.194, f32[512,8]{0,1:T(8,128)S(1)} %max.8, ...), kind=kOutput, calls=%fused_computation.19.clone.1 | convolution fusion | flops 550240256 | bytes 19431936 | tf_op jit(solution)/shard_map/while/body/eval_jaxpr/qhk,khd->qhd/dot_general | solution.py:69
  270.4 8.1 %bitcast_reduce_fusion.5 = (f32[512,8]{0,1:T(8,128)S(1)}, f32[8,512,1024]{2,1,0:T(8,128)}) fusion(bf16[1024,8,64]{0,2,1:T(8,128)(2,1)S(1)} %get-tuple-element.216, bf16[2,512,8,64]{1,3,2,0:T(8,128)(2,1)S(1)} %get-tuple-element.215, s32[]{:T(128)} %get-tuple-element.205), kind=kOutput, calls=%fused_computation.7.clone.1 | convolution fusion | flops 545255424 | bytes 18366468 | tf_op jit(solution)/shard_map/while/body/eval_jaxpr/qhd,khd->qhk/dot_general | solution.py:58
  278.5 2.5 bitcast_reduce_fusion.4
  281.0 0.0 copy-start
  281.0 9.2 %fusion.131 = (f32[512,8]{0,1:T(8,128)S(1)}, f32[512,8]{0,1:T(8,128)S(1)}) fusion(f32[8,512,1024]{2,1,0:T(8,128)S(1)} %get-tuple-element.191, f32[512,8]{0,1:T(8,128)S(1)} %max.8, f32[8,512,1024]{2,1,0:T(8,128)} %get-tuple-element.194), kind=kLoop, calls=%fused_computation.11.clone.1 | loop fusion | flops 25157632 | bytes 33603584 | tf_op jit(solution)/shard_map/while/body/eval_jaxpr/reduce_sum | solution.py:68
  290.2 0.0 copy-done
  290.2 0.0 copy-start.2
  290.2 3.7 %fusion.130 = f32[8,512,64]{1,2,0:T(8,128)S(1)} fusion(bf16[1024,8,64]{0,2,1:T(8,128)(2,1)S(1)} %copy-done, f32[8,512,1024]{2,1,0:T(8,128)S(1)} %get-tuple-element.191, f32[512,8]{0,1:T(8,128)S(1)} %max.8), kind=kOutput, calls=%fused_computation.13.clone.1 | convolution fusion | flops 549453824 | bytes 18890752 | tf_op jit(solution)/shard_map/while/body/eval_jaxpr/qhk,khd->qhd/dot_general | solution.py:75
  293.9 0.0 copy-done.2
  293.9 8.1 %fusion.132 = bf16[2,512,8,64]{1,3,2,0:T(8,128)(2,1)} fusion(bf16[2,512,8,64]{1,3,2,0:T(8,128)(2,1)} %get-tuple-element.206, s32[]{:T(128)} %get-tuple-element.205, f32[8,512,64]{1,2,0:T(8,128)S(1)} %fusion.130, bf16[1024,8,64]{0,2,1:T(8,128)(2,1)S(1)} %copy-done.2, f32[8,512,1024]{2,1,0:T(8,128)} %get-tuple-element.194, f32[512,8]{0,1:T(8,128)S(1)} %max.8, ...), kind=kOutput, calls=%fused_computation.19.clone.1 | convolution fusion | flops 550240256 | bytes 19431936 | tf_op jit(solution)/shard_map/while/body/eval_jaxpr/qhk,khd->qhd/dot_general | solution.py:69
  302.0 2.6 copy.41
  304.7 2.0 reshape.125
  (20 shorter events, 0.2 us)
Async XLA Ops:
  17.8 14.6 %all-to-all-start = ((s32[16,128,1]{1,2,0:T(1,128)}), s32[16,128,1]{1,2,0:T(1,128)S(1)}, u32[]{:S(2)}, u32[]{:S(2)}) async-start(s32[16,128,1]{1,2,0:T(1,128)} %bitcast.9), calls=%async_computation | async-start | bytes 16384 | tf_op jit(solution)/shard_map/all_to_all | solution.py:99
  32.4 47.1 %all-to-all-start.1 = ((bf16[16,128,512]{2,1,0:T(8,128)(2,1)}), bf16[16,128,512]{2,1,0:T(8,128)(2,1)S(1)}, u32[]{:S(2)}, u32[]{:S(2)}) async-start(bf16[16,128,512]{2,1,0:T(8,128)(2,1)} %bitcast.12), calls=%async_computation.1 | async-start | bytes 4194304 | tf_op jit(solution)/shard_map/all_to_all | solution.py:98
  38.4 162.6 %all-gather.2.cloned.1.call-start = ((), (), s32[]{:S(2)}) async-start(), calls=%async_computation.2 | async-start | bytes 3145728 | tf_op jit(solution)/shard_map/all_gather | solution.py:108
  79.5 14.1 %copy-start.3 = (bf16[7,7,512]{2,1,0:T(8,128)(2,1)S(1)}, bf16[7,7,512]{2,1,0:T(8,128)(2,1)}, u32[]{:S(2)}) copy-start(bf16[7,7,512]{2,1,0:T(8,128)(2,1)} %param.11) | copy-start | bytes 150532
  79.5 14.1 %copy-start.4 = (bf16[5,5,512]{2,1,0:T(8,128)(2,1)S(1)}, bf16[5,5,512]{2,1,0:T(8,128)(2,1)}, u32[]{:S(2)}) copy-start(bf16[5,5,512]{2,1,0:T(8,128)(2,1)} %param.12) | copy-start | bytes 76804
  79.5 14.1 %copy-start.5 = (bf16[3,3,512]{2,1,0:T(4,128)(2,1)S(1)}, bf16[3,3,512]{2,1,0:T(4,128)(2,1)}, u32[]{:S(2)}) copy-start(bf16[3,3,512]{2,1,0:T(4,128)(2,1)} %param.13) | copy-start | bytes 27652
  79.5 14.1 %copy-start.6 = (bf16[512]{0:T(512)(128)(2,1)S(1)}, bf16[512]{0:T(512)(128)(2,1)}, u32[]{:S(2)}) copy-start(bf16[512]{0:T(512)(128)(2,1)} %param.14) | copy-start | bytes 3076
  89.3 4.6 %collective-permute-start = (bf16[3,256,512]{2,1,0:T(8,128)(2,1)S(1)}, bf16[3,256,512]{2,1,0:T(8,128)(2,1)S(1)}, u32[]{:S(2)}, u32[]{:S(2)}) collective-permute-start(bf16[3,256,512]{2,1,0:T(8,128)(2,1)S(1)} %bitcast.180), channel_id=1, source_target_pairs={{0,2},{2,4},{4,6},{6,8},{8,10},{10,12},{12,14},{14,16},{16,18},{18... | collective-permute-start | bytes 2359304 | tf_op jit(solution)/shard_map/ppermute | solution.py:20
  92.1 6.4 %collective-permute-start.1 = (bf16[3,256,512]{2,1,0:T(8,128)(2,1)S(1)}, bf16[3,256,512]{2,1,0:T(8,128)(2,1)S(1)}, u32[]{:S(2)}, u32[]{:S(2)}) collective-permute-start(bf16[3,256,512]{2,1,0:T(8,128)(2,1)S(1)} %bitcast.179), channel_id=1, source_target_pairs={{2,0},{4,2},{6,4},{8,6},{10,8},{12,10},{14,12},{16,14},{18,16},{20... | collective-permute-start | bytes 2359304 | tf_op jit(solution)/shard_map/ppermute | solution.py:21
  101.2 47.4 %copy-start.1 = (bf16[1024,3,512]{2,0,1:T(8,128)(2,1)S(1)}, bf16[1024,3,512]{2,0,1:T(8,128)(2,1)}, u32[]{:S(2)}) copy-start(bf16[1024,3,512]{2,0,1:T(8,128)(2,1)} %param.15) | copy-start | bytes 9437188
  208.2 17.0 %collective-permute-start.2 = (bf16[1024,512]{1,0:T(8,128)(2,1)S(1)}, bf16[1024,512]{1,0:T(8,128)(2,1)}, u32[]{:S(2)}, u32[]{:S(2)}) collective-permute-start(bf16[1024,512]{1,0:T(8,128)(2,1)S(1)} %get-tuple-element.85), channel_id=1, source_target_pairs={{30,0},{0,2},{2,4},{4,6},{6,8},{8,10},{10,12},{12,14},{14,16},{16,... | collective-permute-start | bytes 3145736 | tf_op jit(solution)/shard_map/ppermute | solution.py:29
  208.2 28.3 %collective-permute-start.3 = (bf16[1024,512]{1,0:T(8,128)(2,1)}, bf16[1024,512]{1,0:T(8,128)(2,1)}, u32[]{:S(2)}, u32[]{:S(2)}) collective-permute-start(bf16[1024,512]{1,0:T(8,128)(2,1)} %get-tuple-element.84), channel_id=1, source_target_pairs={{30,0},{0,2},{2,4},{4,6},{6,8},{8,10},{10,12},{12,14},{14,16},{16,... | collective-permute-start | bytes 3145736 | tf_op jit(solution)/shard_map/ppermute | solution.py:29
  249.3 9.2 %copy-start = (bf16[1024,8,64]{0,2,1:T(8,128)(2,1)S(1)}, bf16[1024,8,64]{0,2,1:T(8,128)(2,1)}, u32[]{:S(2)}) copy-start(bf16[1024,8,64]{0,2,1:T(8,128)(2,1)} %get-tuple-element.219) | copy-start | bytes 3145732 | tf_op jit(solution)/shard_map/while
  258.6 3.7 %copy-start.2 = (bf16[1024,8,64]{0,2,1:T(8,128)(2,1)S(1)}, bf16[1024,8,64]{0,2,1:T(8,128)(2,1)}, u32[]{:S(2)}) copy-start(bf16[1024,8,64]{0,2,1:T(8,128)(2,1)} %get-tuple-element.218) | copy-start | bytes 3145732 | tf_op jit(solution)/shard_map/while
  281.0 9.2 %copy-start = (bf16[1024,8,64]{0,2,1:T(8,128)(2,1)S(1)}, bf16[1024,8,64]{0,2,1:T(8,128)(2,1)}, u32[]{:S(2)}) copy-start(bf16[1024,8,64]{0,2,1:T(8,128)(2,1)} %get-tuple-element.219) | copy-start | bytes 3145732 | tf_op jit(solution)/shard_map/while
  290.2 3.7 %copy-start.2 = (bf16[1024,8,64]{0,2,1:T(8,128)(2,1)S(1)}, bf16[1024,8,64]{0,2,1:T(8,128)(2,1)}, u32[]{:S(2)}) copy-start(bf16[1024,8,64]{0,2,1:T(8,128)(2,1)} %get-tuple-element.218) | copy-start | bytes 3145732 | tf_op jit(solution)/shard_map/while
Sparse Core Ops, SparseCore 0:
  148.7 52.1 all-gather.1
where the time goes:
time: 314 us
  waiting for transfers between devices  113 us (36%)
  other arithmetic  74.7 us (24%)
  matrix products  50.7 us (16%)
  local copies, waits for them, and re-layouts  42.5 us (14%)
  starting transfers between devices  19.2 us (6%)
  between operations  13.6 us (4%)
    all_gather x1, waiting for transfers between devices, shards(): lax.all_gather(ppeg, 'head', axis=1, tiled=True)  49.3 us
    convert_element_type x1, other arithmetic, mix(): mixed_sum.astype(jnp.bfloat16).reshape(band_rows * width, extended.shape[2])  47.4 us
    all_to_all x1, waiting for transfers between devices, shards(): lax.all_to_all(outgoing, 'seq', split_axis=0, concat_axis=0, tiled=True)  41 us
    reduce_sum x2, other arithmetic, attend_block(): weight_sum = jnp.sum(own_weight, axis=2) + jnp.sum(prior_weight, axis=2)  18.4 us
    ppermute x2, waiting for transfers between devices, passed_along(): return lax.ppermute(block, axis, route)  17.7 us
    dot_general x2, matrix products, attend_block(): jnp.einsum('qhk,khd->qhd', own_weight.astype(jnp.bfloat16), own_values, p...  16.3 us
    dot_general x2, matrix products, attend_block(): jnp.einsum('qhd,khd->qhk', queries, own_keys, preferred_element_type=jnp....  16.2 us
    scatter x1, local copies, waits for them, and re-layouts, shards(): jnp.zeros((tok_dev + 1, local_dim), jnp.bfloat16).at[places].set(arrived)  9.72 us
  transfers between devices with their start and end apart: 7, of which 6 were waited for; matrix products, arithmetic and copies ran while one was open for 6% of the time, Pallas kernels for 0%

commit v1 on v0

v1 whole, which is shorter than its diff:
```python
import functools
import math

import jax
import jax.numpy as jnp
from jax import lax
from jax.experimental import pallas as pl
from jax.experimental.pallas import tpu as pltpu
from jax.sharding import PartitionSpec as P

D = 1024
HEADS = 16
GRID_W = 256
LANES = 128
PAD = 8
STRIP = 64
REACH = 7
HALO = REACH // 2
QUERY_ROWS = 256
MESH = pl.DeviceIdType.MESH
VMEM_BYTES = 56 * 1024 * 1024


def iota(shape, dim):
    return lax.broadcasted_iota(jnp.int32, shape, dim)


def flags(condition):
    return jnp.where(condition, 1.0, 0.0)


def route_kernel(members, capacity, owner_ref, within_ref, features_ref, out_ref, places_ref):
    tok_dev, local_dim = features_ref.shape
    owner = owner_ref[...]
    onehot = flags(iota((members, tok_dev), 0) == owner)
    upper = flags(iota((tok_dev, tok_dev), 0) < iota((tok_dev, tok_dev), 1))
    earlier = jnp.dot(
        onehot.astype(jnp.bfloat16),
        upper.astype(jnp.bfloat16),
        preferred_element_type=jnp.float32,
    )
    rank = jnp.sum(earlier * onehot, axis=0, keepdims=True)
    slot = owner * capacity + rank.astype(jnp.int32)
    within = within_ref[...]
    line = iota((8, tok_dev), 0)
    high = (within >> 8).astype(jnp.float32)
    low = (within & 255).astype(jnp.float32)
    code = jnp.where(line == 0, high, jnp.where(line == 1, low, jnp.where(line == 2, 1.0, 0.0)))
    code = code.astype(jnp.bfloat16)

    def to_band(band, carry):
        pick = flags(iota((capacity, tok_dev), 0) + band * capacity == slot).astype(jnp.bfloat16)
        rows = jnp.dot(pick, features_ref[...], preferred_element_type=jnp.float32)
        rows = rows.astype(jnp.bfloat16)
        for chunk in range(local_dim // LANES):
            out_ref[chunk, band] = rows[:, chunk * LANES : (chunk + 1) * LANES]
        found = lax.dot_general(
            code, pick, (((1,), (1,)), ((), ())), preferred_element_type=jnp.float32
        )
        place = jnp.where(found[2:3] > 0.5, found[0:1] * 256.0 + found[1:2], -1.0)
        places_ref[band] = jnp.broadcast_to(place.astype(jnp.int32), (8, capacity))
        return carry

    lax.fori_loop(0, members, to_band, 0)


def mix_kernel(
    members,
    outgoing_ref,
    places_ref,
    taps_ref,
    bias_ref,
    mixed_ref,
    arrived,
    places_in,
    gather,
    band_bf16,
    halo_up,
    halo_down,
    padded,
    own,
    other,
    out_send,
    out_recv,
    place_send,
    place_recv,
    up_send,
    up_recv,
    down_send,
    down_recv,
    pair_send,
    pair_recv,
):
    chunks, _, capacity, _ = outgoing_ref.shape
    tok_dev = mixed_ref.shape[0]
    local_dim = mixed_ref.shape[1] // 2
    band_rows = tok_dev // GRID_W
    halo_len = HALO * GRID_W
    me = lax.axis_index("seq")
    half = lax.axis_index("head")

    barrier = pltpu.get_barrier_semaphore()

    def greet(step, carry):
        peer = lax.rem(me + step, members)
        pl.semaphore_signal(barrier, inc=1, device_id={"seq": peer}, device_id_type=MESH)
        return carry

    lax.fori_loop(1, members, greet, 0)
    pl.semaphore_signal(barrier, inc=1, device_id={"head": 1 - half}, device_id_type=MESH)
    pl.semaphore_wait(barrier, members)

    def place_copy(peer, slot):
        return pltpu.make_async_remote_copy(
            src_ref=places_ref.at[peer],
            dst_ref=places_in.at[slot],
            send_sem=place_send.at[peer],
            recv_sem=place_recv.at[slot],
            device_id={"seq": peer},
            device_id_type=MESH,
        )

    def token_copy(chunk, peer, slot):
        return pltpu.make_async_remote_copy(
            src_ref=outgoing_ref.at[chunk, peer],
            dst_ref=arrived.at[chunk, slot],
            send_sem=out_send.at[chunk, peer],
            recv_sem=out_recv.at[chunk, slot],
            device_id={"seq": peer},
            device_id_type=MESH,
        )

    def each_peer(action):
        def step_body(step, carry):
            action(lax.rem(me + step, members))
            return carry

        lax.fori_loop(1, members, step_body, 0)

    each_peer(lambda peer: place_copy(peer, me).start())
    for chunk in range(min(2, chunks)):
        each_peer(lambda peer: token_copy(chunk, peer, me).start())

    places_in[pl.ds(me, 1)] = places_ref[pl.ds(me, 1)]
    for chunk in range(chunks):
        arrived[chunk, pl.ds(me, 1)] = outgoing_ref[chunk, pl.ds(me, 1)]
    edge = jnp.zeros((band_rows + 2 * HALO, PAD, LANES), jnp.float32)
    padded[:, 0:PAD, :] = edge
    padded[:, PAD + GRID_W :, :] = edge

    each_peer(lambda peer: place_copy(peer, peer).wait_recv())

    def pick_rows(row, carry):
        start = pl.multiple_of(row * GRID_W, GRID_W)
        cell = iota((GRID_W, capacity), 0) + start
        for source in range(members):
            hit = flags(cell == places_in[source, 0:1, :])
            gather[pl.ds(start, GRID_W), source * capacity : (source + 1) * capacity] = hit.astype(
                jnp.bfloat16
            )
        return carry

    lax.fori_loop(0, band_rows, pick_rows, 0)

    above = lax.rem(me + members - 1, members)
    below = lax.rem(me + 1, members)

    def copy_up(chunk):
        return pltpu.make_async_remote_copy(
            src_ref=band_bf16.at[chunk, pl.ds(0, halo_len)],
            dst_ref=halo_down.at[chunk],
            send_sem=up_send.at[chunk],
            recv_sem=up_recv.at[chunk],
            device_id={"seq": above},
            device_id_type=MESH,
        )

    def copy_down(chunk):
        return pltpu.make_async_remote_copy(
            src_ref=band_bf16.at[chunk, pl.ds(tok_dev - halo_len, halo_len)],
            dst_ref=halo_up.at[chunk],
            send_sem=down_send.at[chunk],
            recv_sem=down_recv.at[chunk],
            device_id={"seq": below},
            device_id_type=MESH,
        )

    def pair_copy(chunk):
        return pltpu.make_async_remote_copy(
            src_ref=own.at[chunk],
            dst_ref=other.at[chunk],
            send_sem=pair_send.at[chunk],
            recv_sem=pair_recv.at[chunk],
            device_id={"head": 1 - half},
            device_id_type=MESH,
        )

    has_above = me > 0
    has_below = me < members - 1

    def place(chunk):
        each_peer(lambda peer: token_copy(chunk, peer, peer).wait_recv())
        tokens = arrived[chunk].reshape(members * capacity, LANES)
        for row in range(band_rows):
            cells = slice(row * GRID_W, (row + 1) * GRID_W)
            found = jnp.dot(gather[cells, :], tokens, preferred_element_type=jnp.float32)
            band_bf16[chunk, cells, :] = found.astype(jnp.bfloat16)

        @pl.when(has_above)
        def _():
            copy_up(chunk).start()

        @pl.when(has_below)
        def _():
            copy_down(chunk).start()

        if chunk + 2 < chunks:
            each_peer(lambda peer: token_copy(chunk, peer, me).wait_send())
            each_peer(lambda peer: token_copy(chunk + 2, peer, me).start())

    def convolve(chunk):
        for row in range(band_rows):
            padded[HALO + row, PAD : PAD + GRID_W, :] = band_bf16[
                chunk, row * GRID_W : (row + 1) * GRID_W, :
            ].astype(jnp.float32)

        blank = jnp.zeros((HALO, GRID_W, LANES), jnp.float32)

        @pl.when(has_above)
        def _():
            copy_down(chunk).wait_recv()
            for row in range(HALO):
                padded[row, PAD : PAD + GRID_W, :] = halo_up[
                    chunk, row * GRID_W : (row + 1) * GRID_W, :
                ].astype(jnp.float32)

        @pl.when(jnp.logical_not(has_above))
        def _():
            padded[0:HALO, PAD : PAD + GRID_W, :] = blank

        @pl.when(has_below)
        def _():
            copy_up(chunk).wait_recv()
            for row in range(HALO):
                padded[HALO + band_rows + row, PAD : PAD + GRID_W, :] = halo_down[
                    chunk, row * GRID_W : (row + 1) * GRID_W, :
                ].astype(jnp.float32)

        @pl.when(jnp.logical_not(has_below))
        def _():
            padded[HALO + band_rows :, PAD : PAD + GRID_W, :] = blank

        lanes = slice(chunk * LANES, (chunk + 1) * LANES)
        columns = pl.ds(pl.multiple_of(half * local_dim + chunk * LANES, LANES), LANES)

        def strip(index, carry):
            start = pl.multiple_of(index * STRIP, STRIP)
            sums = [jnp.broadcast_to(bias_ref[:, lanes], (STRIP, LANES))] * band_rows
            for j in range(REACH):
                for line in range(band_rows + 2 * HALO):
                    cells = padded[line, pl.ds(start + (PAD - HALO + j), STRIP), :]
                    for row in range(max(0, line - 2 * HALO), min(band_rows, line + 1)):
                        tap = (line - row) * REACH + j
                        sums[row] = sums[row] + cells * taps_ref[tap : tap + 1, lanes]
            for row in range(band_rows):
                value = sums[row].astype(jnp.bfloat16)
                where = pl.ds(pl.multiple_of(row * GRID_W + start, STRIP), STRIP)
                own[chunk, where, :] = value
                mixed_ref[where, columns] = value
            return carry

        lax.fori_loop(0, GRID_W // STRIP, strip, 0)
        pair_copy(chunk).start()

    for chunk in range(chunks + 1):
        if chunk < chunks:
            place(chunk)
        if chunk > 0:
            convolve(chunk - 1)

    for chunk in range(chunks):
        pair_copy(chunk).wait_recv()
        columns = pl.ds(pl.multiple_of((1 - half) * local_dim + chunk * LANES, LANES), LANES)
        mixed_ref[:, columns] = other[chunk]

    each_peer(lambda peer: place_copy(peer, me).wait_send())
    for chunk in range(chunks):
        pair_copy(chunk).wait_send()
        if chunk + 2 >= chunks:
            each_peer(lambda peer: token_copy(chunk, peer, me).wait_send())

        @pl.when(has_above)
        def _():
            copy_up(chunk).wait_send()

        @pl.when(has_below)
        def _():
            copy_down(chunk).wait_send()


def attend_kernel(
    members, head_dim, mixed_ref, weights_ref, out_ref, queries, kept, prior, top, numer, denom, send, recv
):
    tok_dev = mixed_ref.shape[0]
    local_dim = weights_ref.shape[1] // 3
    chunks = local_dim // LANES
    me = lax.axis_index("seq")
    above = lax.rem(me + members - 1, members)
    below = lax.rem(me + 1, members)
    scale = 1.0 / math.sqrt(head_dim)

    barrier = pltpu.get_barrier_semaphore()
    for neighbour in (above, below):
        pl.semaphore_signal(barrier, inc=1, device_id={"seq": neighbour}, device_id_type=MESH)
    pl.semaphore_wait(barrier, 2)

    def band_copy(chunk):
        return pltpu.make_async_remote_copy(
            src_ref=kept.at[chunk],
            dst_ref=prior.at[chunk],
            send_sem=send.at[chunk],
            recv_sem=recv.at[chunk],
            device_id={"seq": below},
            device_id_type=MESH,
        )

    blocks = tok_dev // QUERY_ROWS

    for chunk in range(chunks):
        for kind in range(2):
            first = (kind + 1) * local_dim + chunk * LANES
            part = weights_ref[:, first : first + LANES]

            def project(index, carry):
                rows = pl.ds(pl.multiple_of(index * QUERY_ROWS, QUERY_ROWS), QUERY_ROWS)
                kept[chunk, kind, rows, :] = jnp.dot(
                    mixed_ref[rows, :], part, preferred_element_type=jnp.float32
                ).astype(jnp.bfloat16)
                return carry

            lax.fori_loop(0, blocks, project, 0)
        band_copy(chunk).start()

    def project_queries(index, carry):
        rows = pl.ds(pl.multiple_of(index * QUERY_ROWS, QUERY_ROWS), QUERY_ROWS)
        product = jnp.dot(
            mixed_ref[rows, :], weights_ref[:, :local_dim], preferred_element_type=jnp.float32
        ).astype(jnp.bfloat16)
        for chunk in range(chunks):
            queries[chunk, rows, :] = product[:, chunk * LANES : (chunk + 1) * LANES] * jnp.asarray(
                scale, jnp.bfloat16
            )
        return carry

    lax.fori_loop(0, blocks, project_queries, 0)

    def partial(chunk, block_rows, source):
        query = queries[chunk, block_rows, :]
        lane_q = iota(query.shape, 1)
        keys = source[chunk, 0]
        values = source[chunk, 1]
        lane_v = iota(values.shape, 1)
        peak = total = summed = None
        for head in range(LANES // head_dim):
            mine_q = lane_q // head_dim == head
            mine_v = lane_v // head_dim == head
            score = lax.dot_general(
                jnp.where(mine_q, query, jnp.zeros_like(query)),
                keys,
                (((1,), (1,)), ((), ())),
                preferred_element_type=jnp.float32,
            )
            high = jnp.max(score, axis=1, keepdims=True)
            probs = jnp.exp(score - high).astype(jnp.bfloat16)
            both = jnp.dot(
                probs,
                jnp.where(mine_v, values, jnp.ones_like(values)),
                preferred_element_type=jnp.float32,
            )
            swapped = pltpu.roll(both, head_dim, 1)
            high = jnp.broadcast_to(high, both.shape)
            if head == 0:
                peak, total, summed = high, swapped, both
            else:
                peak = jnp.where(mine_q, high, peak)
                total = jnp.where(mine_q, swapped, total)
                summed = jnp.where(mine_q, both, summed)
        return peak, total, summed

    for chunk in range(chunks):

        def attend_own(index, carry):
            rows = pl.ds(pl.multiple_of(index * QUERY_ROWS, QUERY_ROWS), QUERY_ROWS)
            peak, total, summed = partial(chunk, rows, kept)
            top[chunk, rows, :] = peak
            denom[chunk, rows, :] = total
            numer[chunk, rows, :] = summed
            return carry

        lax.fori_loop(0, blocks, attend_own, 0)

    for chunk in range(chunks):
        band_copy(chunk).wait_recv()

        def attend_prior(index, carry):
            rows = pl.ds(pl.multiple_of(index * QUERY_ROWS, QUERY_ROWS), QUERY_ROWS)
            peak, total, summed = partial(chunk, rows, prior)
            before = top[chunk, rows, :]
            high = jnp.maximum(peak, before)
            here = jnp.exp(peak - high)
            there = jnp.exp(before - high)
            total = total * here + denom[chunk, rows, :] * there
            summed = summed * here + numer[chunk, rows, :] * there
            out_ref[rows, chunk * LANES : (chunk + 1) * LANES] = (summed / total).astype(jnp.bfloat16)
            return carry

        lax.fori_loop(0, blocks, attend_prior, 0)

    for chunk in range(chunks):
        band_copy(chunk).wait_send()


def shards(features, cells, conv7, conv5, conv3, conv_bias, w_qkv):
    tok_dev, local_dim = features.shape
    members = lax.axis_size("seq")
    capacity = 2 * tok_dev // members
    chunks = local_dim // LANES
    head_dim = D // HEADS
    band_rows = tok_dev // GRID_W
    halo_len = HALO * GRID_W
    vmem = pl.BlockSpec(memory_space=pltpu.VMEM)
    dma = pltpu.SemaphoreType.DMA

    owner = (cells // tok_dev).reshape(1, tok_dev)
    within = cells.reshape(1, tok_dev) - owner * tok_dev
    outgoing, places = pl.pallas_call(
        functools.partial(route_kernel, members, capacity),
        out_shape=(
            jax.ShapeDtypeStruct((chunks, members, capacity, LANES), jnp.bfloat16),
            jax.ShapeDtypeStruct((members, 8, capacity), jnp.int32),
        ),
        in_specs=[vmem] * 3,
        out_specs=(vmem, vmem),
        compiler_params=pltpu.CompilerParams(vmem_limit_bytes=VMEM_BYTES),
        name="route",
    )(owner, within, features)

    merged = conv7.astype(jnp.float32) + jnp.pad(
        conv5.astype(jnp.float32), ((1, 1), (1, 1), (0, 0))
    )
    merged = merged + jnp.pad(conv3.astype(jnp.float32), ((2, 2), (2, 2), (0, 0)))
    merged = merged + jnp.pad(jnp.ones((1, 1, local_dim), jnp.float32), ((3, 3), (3, 3), (0, 0)))
    taps = merged.reshape(REACH * REACH, local_dim)
    bias = conv_bias.astype(jnp.float32).reshape(1, local_dim)

    mixed = pl.pallas_call(
        functools.partial(mix_kernel, members),
        out_shape=jax.ShapeDtypeStruct((tok_dev, 2 * local_dim), jnp.bfloat16),
        in_specs=[vmem] * 4,
        out_specs=vmem,
        scratch_shapes=[
            pltpu.VMEM((chunks, members, capacity, LANES), jnp.bfloat16),
            pltpu.VMEM((members, 8, capacity), jnp.int32),
            pltpu.VMEM((tok_dev, members * capacity), jnp.bfloat16),
            pltpu.VMEM((chunks, tok_dev, LANES), jnp.bfloat16),
            pltpu.VMEM((chunks, halo_len, LANES), jnp.bfloat16),
            pltpu.VMEM((chunks, halo_len, LANES), jnp.bfloat16),
            pltpu.VMEM((band_rows + 2 * HALO, GRID_W + 2 * PAD, LANES), jnp.float32),
            pltpu.VMEM((chunks, tok_dev, LANES), jnp.bfloat16),
            pltpu.VMEM((chunks, tok_dev, LANES), jnp.bfloat16),
            dma((chunks, members)),
            dma((chunks, members)),
            dma((members,)),
            dma((members,)),
            dma((chunks,)),
            dma((chunks,)),
            dma((chunks,)),
            dma((chunks,)),
            dma((chunks,)),
            dma((chunks,)),
        ],
        compiler_params=pltpu.CompilerParams(
            collective_id=0, has_side_effects=True, vmem_limit_bytes=VMEM_BYTES
        ),
        name="mix",
    )(outgoing, places, taps, bias)

    weights = w_qkv.reshape(w_qkv.shape[0], 3 * local_dim)
    return pl.pallas_call(
        functools.partial(attend_kernel, members, head_dim),
        out_shape=jax.ShapeDtypeStruct((tok_dev, local_dim), jnp.bfloat16),
        in_specs=[vmem] * 2,
        out_specs=vmem,
        scratch_shapes=[
            pltpu.VMEM((chunks, tok_dev, LANES), jnp.bfloat16),
            pltpu.VMEM((chunks, 2, tok_dev, LANES), jnp.bfloat16),
            pltpu.VMEM((chunks, 2, tok_dev, LANES), jnp.bfloat16),
            pltpu.VMEM((chunks, tok_dev, LANES), jnp.float32),
            pltpu.VMEM((chunks, tok_dev, LANES), jnp.float32),
            pltpu.VMEM((chunks, tok_dev, LANES), jnp.float32),
            dma((chunks,)),
            dma((chunks,)),
        ],
        compiler_params=pltpu.CompilerParams(
            collective_id=1, has_side_effects=True, vmem_limit_bytes=VMEM_BYTES
        ),
        name="attend",
    )(mixed, weights)


def solution(mesh):
    placed = (
        P("seq", "head"),
        P("seq"),
        P(None, None, "head"),
        P(None, None, "head"),
        P(None, None, "head"),
        P("head"),
        P(None, None, "head"),
    )
    return jax.shard_map(
        shards, mesh=mesh, in_specs=placed, out_specs=P("seq", "head"), check_vma=False
    )
```

time: 314 us -> 155 us (0.49)
  Pallas kernels: 0 us -> 142 us
  waiting for transfers between devices: 113 us -> 0 us
  other arithmetic: 74.7 us -> 3.48 us
  matrix products: 50.7 us -> 0 us
  local copies, waits for them, and re-layouts: 42.5 us -> 9.06 us
  starting transfers between devices: 19.2 us -> 0 us
  between operations: 13.6 us -> 0.03 us
    pallas_call x0 -> x3, Pallas kernels: none -> 142 us  [the longest x1 77.5 us: shards(): pl.pallas_call(functools.partial(mix_kernel, members), out_shape=jax.Shap...]
    dot_general x9 -> x0, matrix products: 50.7 us -> none  [the longest x2 16.3 us: attend_block(): jnp.einsum('qhk,khd->qhd', own_weight.astype(jnp.bfloat16), own_values, p...]
    convert_element_type x4 -> x0, other arithmetic: 50.2 us -> none  [the longest x1 47.4 us: mix(): mixed_sum.astype(jnp.bfloat16).reshape(band_rows * width, extended.shape[2])]
    all_gather x1 -> x0, waiting for transfers between devices: 49.3 us -> none  [shards(): lax.all_gather(ppeg, 'head', axis=1, tiled=True)]
    all_to_all x2 -> x0, waiting for transfers between devices: 41 us -> none  [the longest x1 41 us: shards(): lax.all_to_all(outgoing, 'seq', split_axis=0, concat_axis=0, tiled=True)]
    ppermute x4 -> x0, waiting for transfers between devices: 22.3 us -> none  [the longest x2 17.7 us: passed_along(): return lax.ppermute(block, axis, route)]
    scatter x3 -> x0, local copies, waits for them, and re-layouts: 21.8 us -> none  [the longest x1 9.72 us: shards(): jnp.zeros((tok_dev + 1, local_dim), jnp.bfloat16).at[places].set(arrived)]
    reduce_sum x3 -> x0, other arithmetic: 18.4 us -> none  [the longest x2 18.4 us: attend_block(): weight_sum = jnp.sum(own_weight, axis=2) + jnp.sum(prior_weight, axis=2)]
  transfers between devices with their start and end apart: 7 -> 0, of which waited for: 6 -> 0; matrix products, arithmetic and copies ran while one was open for 6% -> 0% of each run, Pallas kernels for 0% -> 0%
where the time goes in v1:
time: 155 us; the launch traced here: 154 us
  Pallas kernels  142 us (92%)
  local copies, waits for them, and re-layouts  9.06 us (6%)
  other arithmetic  3.48 us (2%)
    pallas_call x1, Pallas kernels, shards(): pl.pallas_call(functools.partial(mix_kernel, members), out_shape=jax.Shap...  77.5 us
    pallas_call x1, Pallas kernels, shards(): pl.pallas_call(functools.partial(attend_kernel, members, head_dim), out_s...  55.5 us
    pallas_call x1, Pallas kernels, shards(): pl.pallas_call(functools.partial(route_kernel, members, capacity), out_sh...  8.62 us
    unnamed x2, local copies, waits for them, and re-layouts  5.45 us

profile of v1, /device:TPU:0, one launch (start us, length us, event | category | flops | bytes accessed | tf_op | source)
XLA Modules:
  0.0 154.2 jit_solution(10390377641428012467)
XLA Ops:
  0.0 1.3 reshape.23
  1.3 1.3 multiply_subtract_fusion
  2.6 0.9 add_add_fusion
  3.5 0.7 reshape.19.taps_ref
  4.1 8.6 %route.1 = (bf16[4,16,128,128]{3,2,1,0:T(8,128)(2,1)}, s32[16,8,128]{2,1,0:T(8,128)}) custom-call(s32[1,1024]{1,0:T(1,128)} %bitcast.6, s32[1,1024]{1,0:T(1,128)} %bitcast.5, bf16[1024,512]{1,0:T(8,128)(2,1)} %features_ref.1), custom_call_target="tpu_custom_call" | custom-call | tf_op jit(solution)/shard_map/route/pallas_call | solution.py:436
  12.8 77.5 %mix.1.mixed_ref = bf16[1024,1024]{1,0:T(8,128)(2,1)} custom-call(bf16[4,16,128,128]{3,2,1,0:T(8,128)(2,1)} %get-tuple-element.7.outgoing_ref, s32[16,8,128]{2,1,0:T(8,128)} %get-tuple-element.8.places_ref, f32[49,512]{1,0:T(8,128)} %reshape.19.taps_ref, f32[1,512]{1,0:T(1,128)} %bitcast.7), custom_call_target="tpu_custom_call" | custom-call | tf_op jit(solution)/shard_map/mix/pallas_call | solution.py:456
  90.3 3.2 %copy.9 = bf16[1024,3,512]{0,2,1:T(8,128)(2,1)S(1)} copy(bf16[1024,3,512]{2,0,1:T(8,128)(2,1)} %param.13) | data formatting | bytes 6291456 | tf_op args[6]
  93.5 2.9 %copy.10.weights_ref = bf16[1024,1536]{1,0:T(8,128)(2,1)} copy(bf16[1024,1536]{0,1:T(8,128)(2,1)S(1)} %bitcast.4) | data formatting | bytes 6291456 | tf_op jit(solution)/shard_map/reshape | solution.py:488
  96.4 55.5 %attend.1 = bf16[1024,512]{1,0:T(8,128)(2,1)} custom-call(bf16[1024,1024]{1,0:T(8,128)(2,1)} %mix.1.mixed_ref, bf16[1024,1536]{1,0:T(8,128)(2,1)} %copy.10.weights_ref), custom_call_target="tpu_custom_call" | custom-call | tf_op jit(solution)/shard_map/attend/pallas_call | solution.py:489
  151.9 2.3 %copy.12 = bf16[1024,512]{1,0:T(8,128)(2,1)} copy(bf16[1024,512]{1,0:T(8,128)(2,1)} %attend.1) | data formatting | bytes 2097152

commit v2 on v1

v2 whole, which is shorter than its diff:
```python
import functools
import math

import jax
import jax.numpy as jnp
from jax import lax
from jax.experimental import pallas as pl
from jax.experimental.pallas import tpu as pltpu
from jax.sharding import PartitionSpec as P

D = 1024
HEADS = 16
GRID_W = 256
LANES = 128
PAD = 8
STRIP = 32
REACH = 7
HALO = REACH // 2
QUERY_ROWS = 512
MESH = pl.DeviceIdType.MESH
VMEM_BYTES = 56 * 1024 * 1024


def iota(shape, dim):
    return lax.broadcasted_iota(jnp.int32, shape, dim)


def flags(condition):
    return jnp.where(condition, 1.0, 0.0)


def band_kernel(
    members,
    head_dim,
    cells_ref,
    features_ref,
    weights_hbm,
    taps_ref,
    bias_ref,
    out_ref,
    outgoing_ref,
    places_ref,
    mixed_ref,
    arrived,
    places_in,
    gather,
    band_bf16,
    halo_up,
    halo_down,
    padded,
    weights_ref,
    queries,
    keys_own,
    values_own,
    keys_prior,
    values_prior,
    top,
    numer,
    denom,
    weight_sem,
    out_send,
    out_recv,
    place_send,
    place_recv,
    up_send,
    up_recv,
    down_send,
    down_recv,
    pair_send,
    pair_recv,
    key_send,
    key_recv,
    value_send,
    value_recv,
):
    chunks, _, capacity, _ = outgoing_ref.shape
    fetch = pltpu.make_async_copy(weights_hbm, weights_ref, weight_sem)
    fetch.start()
    tok_dev, local_dim = out_ref.shape
    band_rows = tok_dev // GRID_W
    halo_len = HALO * GRID_W
    me = lax.axis_index("seq")
    half = lax.axis_index("head")

    barrier = pltpu.get_barrier_semaphore()

    def greet(step, carry):
        peer = lax.rem(me + step, members)
        pl.semaphore_signal(barrier, inc=1, device_id={"seq": peer}, device_id_type=MESH)
        return carry

    lax.fori_loop(1, members, greet, 0)
    pl.semaphore_signal(barrier, inc=1, device_id={"head": 1 - half}, device_id_type=MESH)
    pl.semaphore_wait(barrier, members)

    def place_copy(peer, slot):
        return pltpu.make_async_remote_copy(
            src_ref=places_ref.at[peer],
            dst_ref=places_in.at[slot],
            send_sem=place_send.at[peer],
            recv_sem=place_recv.at[slot],
            device_id={"seq": peer},
            device_id_type=MESH,
        )

    def token_copy(chunk, peer, slot):
        return pltpu.make_async_remote_copy(
            src_ref=outgoing_ref.at[chunk, peer],
            dst_ref=arrived.at[chunk, slot],
            send_sem=out_send.at[chunk, peer],
            recv_sem=out_recv.at[chunk, slot],
            device_id={"seq": peer},
            device_id_type=MESH,
        )

    def each_peer(action):
        def step_body(step, carry):
            away = (step + 1) // 2
            shift = members // 2 + lax.select(lax.rem(step, 2) == 1, away, -away)
            action(lax.rem(me + shift, members))
            return carry

        lax.fori_loop(0, members - 1, step_body, 0)

    cells = cells_ref[...]
    owner = ((cells.astype(jnp.float32) + 0.5) * (1.0 / tok_dev)).astype(jnp.int32)
    within = cells - owner * tok_dev
    onehot = flags(iota((members, tok_dev), 0) == owner)
    upper = flags(iota((tok_dev, tok_dev), 0) < iota((tok_dev, tok_dev), 1))
    earlier = jnp.dot(
        onehot.astype(jnp.bfloat16),
        upper.astype(jnp.bfloat16),
        preferred_element_type=jnp.float32,
    )
    rank = jnp.sum(earlier * onehot, axis=0, keepdims=True)
    slot = owner * capacity + rank.astype(jnp.int32)
    line = iota((8, tok_dev), 0)
    high = (within >> 8).astype(jnp.float32)
    low = (within & 255).astype(jnp.float32)
    code = jnp.where(line == 0, high, jnp.where(line == 1, low, jnp.where(line == 2, 1.0, 0.0)))
    code = code.astype(jnp.bfloat16)

    def pack(band):
        pick = flags(iota((capacity, tok_dev), 0) + band * capacity == slot).astype(jnp.bfloat16)
        rows = jnp.dot(pick, features_ref[...], preferred_element_type=jnp.float32)
        rows = rows.astype(jnp.bfloat16)
        for chunk in range(chunks):
            outgoing_ref[chunk, band] = rows[:, chunk * LANES : (chunk + 1) * LANES]
        found = lax.dot_general(
            code, pick, (((1,), (1,)), ((), ())), preferred_element_type=jnp.float32
        )
        spot = jnp.where(found[2:3] > 0.5, found[0:1] * 256.0 + found[1:2], -1.0)
        places_ref[band] = jnp.broadcast_to(spot.astype(jnp.int32), (8, capacity))

    def pack_and_send(peer):
        pack(peer)
        place_copy(peer, me).start()
        token_copy(0, peer, me).start()

    each_peer(pack_and_send)
    if chunks > 1:
        each_peer(lambda peer: token_copy(1, peer, me).start())
    pack(me)

    places_in[pl.ds(me, 1)] = places_ref[pl.ds(me, 1)]
    for chunk in range(chunks):
        arrived[chunk, pl.ds(me, 1)] = outgoing_ref[chunk, pl.ds(me, 1)]
    edge = jnp.zeros((band_rows + 2 * HALO, PAD, LANES), jnp.float32)
    padded[:, 0:PAD, :] = edge
    padded[:, PAD + GRID_W :, :] = edge

    each_peer(lambda peer: place_copy(peer, peer).wait_recv())

    def pick_rows(row, carry):
        start = pl.multiple_of(row * GRID_W, GRID_W)
        cell = iota((GRID_W, capacity), 0) + start
        for source in range(members):
            hit = flags(cell == places_in[source, 0:1, :])
            gather[pl.ds(start, GRID_W), source * capacity : (source + 1) * capacity] = hit.astype(
                jnp.bfloat16
            )
        return carry

    lax.fori_loop(0, band_rows, pick_rows, 0)

    above = lax.rem(me + members - 1, members)
    below = lax.rem(me + 1, members)

    def copy_up(chunk):
        return pltpu.make_async_remote_copy(
            src_ref=band_bf16.at[chunk, pl.ds(0, halo_len)],
            dst_ref=halo_down.at[chunk],
            send_sem=up_send.at[chunk],
            recv_sem=up_recv.at[chunk],
            device_id={"seq": above},
            device_id_type=MESH,
        )

    def copy_down(chunk):
        return pltpu.make_async_remote_copy(
            src_ref=band_bf16.at[chunk, pl.ds(tok_dev - halo_len, halo_len)],
            dst_ref=halo_up.at[chunk],
            send_sem=down_send.at[chunk],
            recv_sem=down_recv.at[chunk],
            device_id={"seq": below},
            device_id_type=MESH,
        )

    def own_columns(chunk):
        return pl.ds(pl.multiple_of(half * local_dim + chunk * LANES, LANES), LANES)

    def pair_copy(chunk):
        return pltpu.make_async_remote_copy(
            src_ref=mixed_ref.at[:, own_columns(chunk)],
            dst_ref=mixed_ref.at[:, own_columns(chunk)],
            send_sem=pair_send.at[chunk],
            recv_sem=pair_recv.at[chunk],
            device_id={"head": 1 - half},
            device_id_type=MESH,
        )

    has_above = me > 0
    has_below = me < members - 1

    def place(chunk):
        each_peer(lambda peer: token_copy(chunk, peer, peer).wait_recv())
        tokens = arrived[chunk].reshape(members * capacity, LANES)
        for row in range(band_rows):
            cells = slice(row * GRID_W, (row + 1) * GRID_W)
            found = jnp.dot(gather[cells, :], tokens, preferred_element_type=jnp.float32)
            band_bf16[chunk, cells, :] = found.astype(jnp.bfloat16)

        @pl.when(has_above)
        def _():
            copy_up(chunk).start()

        @pl.when(has_below)
        def _():
            copy_down(chunk).start()

        if chunk + 2 < chunks:
            each_peer(lambda peer: token_copy(chunk, peer, me).wait_send())
            each_peer(lambda peer: token_copy(chunk + 2, peer, me).start())

    def convolve(chunk):
        for row in range(band_rows):
            padded[HALO + row, PAD : PAD + GRID_W, :] = band_bf16[
                chunk, row * GRID_W : (row + 1) * GRID_W, :
            ].astype(jnp.float32)

        blank = jnp.zeros((HALO, GRID_W, LANES), jnp.float32)

        @pl.when(has_above)
        def _():
            copy_down(chunk).wait_recv()
            for row in range(HALO):
                padded[row, PAD : PAD + GRID_W, :] = halo_up[
                    chunk, row * GRID_W : (row + 1) * GRID_W, :
                ].astype(jnp.float32)

        @pl.when(jnp.logical_not(has_above))
        def _():
            padded[0:HALO, PAD : PAD + GRID_W, :] = blank

        @pl.when(has_below)
        def _():
            copy_up(chunk).wait_recv()
            for row in range(HALO):
                padded[HALO + band_rows + row, PAD : PAD + GRID_W, :] = halo_down[
                    chunk, row * GRID_W : (row + 1) * GRID_W, :
                ].astype(jnp.float32)

        @pl.when(jnp.logical_not(has_below))
        def _():
            padded[HALO + band_rows :, PAD : PAD + GRID_W, :] = blank

        lanes = slice(chunk * LANES, (chunk + 1) * LANES)
        columns = own_columns(chunk)

        def strip(index, carry):
            start = pl.multiple_of(index * STRIP, STRIP)
            sums = [jnp.broadcast_to(bias_ref[:, lanes], (STRIP, LANES))] * band_rows
            for j in range(REACH):
                taps = [taps_ref[i * REACH + j : i * REACH + j + 1, lanes] for i in range(REACH)]
                for line in range(band_rows + 2 * HALO):
                    cells = padded[line, pl.ds(start + (PAD - HALO + j), STRIP), :]
                    for row in range(max(0, line - 2 * HALO), min(band_rows, line + 1)):
                        sums[row] = sums[row] + cells * taps[line - row]
            for row in range(band_rows):
                value = sums[row].astype(jnp.bfloat16)
                where = pl.ds(pl.multiple_of(row * GRID_W + start, STRIP), STRIP)
                mixed_ref[where, columns] = value
            return carry

        lax.fori_loop(0, GRID_W // STRIP, strip, 0)
        pair_copy(chunk).start()

    for chunk in range(chunks + 1):
        if chunk < chunks:
            place(chunk)
        if chunk > 0:
            convolve(chunk - 1)

    fetch.wait()
    for chunk in range(chunks):
        pair_copy(chunk).wait_recv()

    def key_copy(chunk):
        return pltpu.make_async_remote_copy(
            src_ref=keys_own.at[chunk],
            dst_ref=keys_prior.at[chunk],
            send_sem=key_send.at[chunk],
            recv_sem=key_recv.at[chunk],
            device_id={"seq": below},
            device_id_type=MESH,
        )

    def value_copy(chunk):
        return pltpu.make_async_remote_copy(
            src_ref=values_own.at[chunk],
            dst_ref=values_prior.at[chunk],
            send_sem=value_send.at[chunk],
            recv_sem=value_recv.at[chunk],
            device_id={"seq": below},
            device_id_type=MESH,
        )

    blocks = tok_dev // QUERY_ROWS

    def block_of(index):
        return pl.ds(pl.multiple_of(index * QUERY_ROWS, QUERY_ROWS), QUERY_ROWS)

    def project_keys(index, carry):
        rows = block_of(index)
        product = jnp.dot(
            mixed_ref[rows, :], weights_ref[:, local_dim:], preferred_element_type=jnp.float32
        )
        for chunk in range(chunks):
            first = chunk * LANES
            keys = jnp.transpose(product[:, first : first + LANES])
            keys_own[chunk, :, rows] = keys.astype(jnp.bfloat16)
            first = local_dim + first
            values_own[chunk, rows, :] = product[:, first : first + LANES].astype(jnp.bfloat16)
        return carry

    lax.fori_loop(0, blocks, project_keys, 0)
    for chunk in range(chunks):
        key_copy(chunk).start()
        value_copy(chunk).start()

    heads = LANES // head_dim
    lane_q = iota((QUERY_ROWS, LANES), 1) // head_dim
    lane_v = iota((tok_dev, LANES), 1) // head_dim
    log_scale = math.log2(math.e) / math.sqrt(head_dim)

    def project_queries(index, carry):
        rows = block_of(index)
        product = jnp.dot(
            mixed_ref[rows, :], weights_ref[:, :local_dim], preferred_element_type=jnp.float32
        ).astype(jnp.bfloat16)
        for chunk in range(chunks):
            query = product[:, chunk * LANES : (chunk + 1) * LANES].astype(jnp.float32) * log_scale
            coarse = query.astype(jnp.bfloat16).astype(jnp.float32)
            fine = pltpu.roll(query - coarse, head_dim, 1)
            for head in range(heads):
                queries[chunk, head, rows, :] = jnp.where(lane_q == head, coarse, fine).astype(
                    jnp.bfloat16
                )
        return carry

    lax.fori_loop(0, blocks, project_queries, 0)

    def partial(chunk, rows, keys_ref, values_ref):
        values = values_ref[chunk]
        scores = []
        for head in range(heads):
            keys = keys_ref[chunk, head * head_dim : (head + 1) * head_dim, :]
            scores.append(
                jnp.dot(
                    queries[chunk, head, rows, :],
                    jnp.concatenate([keys] * heads, axis=0),
                    preferred_element_type=jnp.float32,
                )
            )
        peaks = [jnp.max(score, axis=1, keepdims=True) for score in scores]
        pairs = []
        for head in range(heads):
            probs = jnp.exp2(scores[head] - peaks[head]).astype(jnp.bfloat16)
            pairs.append(
                jnp.dot(
                    probs,
                    jnp.where(lane_v == head, values, jnp.ones_like(values)),
                    preferred_element_type=jnp.float32,
                )
            )
        first = lane_q == 0
        peak = jnp.where(first, peaks[0], peaks[1])
        summed = jnp.where(first, pairs[0], pairs[1])
        total = pltpu.roll(jnp.where(first, pairs[1], pairs[0]), head_dim, 1)
        return peak, total, summed

    def own_chunk(chunk, carry):
        def attend_own(index, inner):
            rows = block_of(index)
            peak, total, summed = partial(chunk, rows, keys_own, values_own)
            top[chunk, rows, :] = peak
            denom[chunk, rows, :] = total
            numer[chunk, rows, :] = summed
            return inner

        return lax.fori_loop(0, blocks, attend_own, carry)

    lax.fori_loop(0, chunks, own_chunk, 0)

    def prior_chunk(chunk, carry):
        key_copy(chunk).wait_recv()
        value_copy(chunk).wait_recv()

        def attend_prior(index, inner):
            rows = block_of(index)
            peak, total, summed = partial(chunk, rows, keys_prior, values_prior)
            before = top[chunk, rows, :]
            high = jnp.maximum(peak, before)
            here = jnp.exp2(peak - high)
            there = jnp.exp2(before - high)
            total = total * here + denom[chunk, rows, :] * there
            summed = summed * here + numer[chunk, rows, :] * there
            columns = pl.ds(pl.multiple_of(chunk * LANES, LANES), LANES)
            out_ref[rows, columns] = (summed / total).astype(jnp.bfloat16)
            return inner

        return lax.fori_loop(0, blocks, attend_prior, carry)

    lax.fori_loop(0, chunks, prior_chunk, 0)

    each_peer(lambda peer: place_copy(peer, me).wait_send())
    for chunk in range(chunks):
        pair_copy(chunk).wait_send()
        if chunk + 2 >= chunks:
            each_peer(lambda peer: token_copy(chunk, peer, me).wait_send())

        @pl.when(has_above)
        def _():
            copy_up(chunk).wait_send()

        @pl.when(has_below)
        def _():
            copy_down(chunk).wait_send()

    for chunk in range(chunks):
        key_copy(chunk).wait_send()
        value_copy(chunk).wait_send()


def shards(features, cells, conv7, conv5, conv3, conv_bias, w_qkv):
    tok_dev, local_dim = features.shape
    members = lax.axis_size("seq")
    capacity = 2 * tok_dev // members
    chunks = local_dim // LANES
    head_dim = D // HEADS
    band_rows = tok_dev // GRID_W
    halo_len = HALO * GRID_W
    vmem = pl.BlockSpec(memory_space=pltpu.VMEM)
    dma = pltpu.SemaphoreType.DMA

    merged = conv7.astype(jnp.float32) + jnp.pad(
        conv5.astype(jnp.float32), ((1, 1), (1, 1), (0, 0))
    )
    merged = merged + jnp.pad(conv3.astype(jnp.float32), ((2, 2), (2, 2), (0, 0)))
    merged = merged + jnp.pad(jnp.ones((1, 1, local_dim), jnp.float32), ((3, 3), (3, 3), (0, 0)))
    taps = merged.reshape(REACH * REACH, local_dim)
    bias = conv_bias.astype(jnp.float32).reshape(1, local_dim)

    weights = w_qkv.reshape(w_qkv.shape[0], 3 * local_dim)
    half_words = functools.partial(pltpu.VMEM, dtype=jnp.bfloat16)
    words = functools.partial(pltpu.VMEM, dtype=jnp.float32)
    return pl.pallas_call(
        functools.partial(band_kernel, members, head_dim),
        out_shape=jax.ShapeDtypeStruct((tok_dev, local_dim), jnp.bfloat16),
        in_specs=[vmem, vmem, pl.BlockSpec(memory_space=pl.ANY), vmem, vmem],
        out_specs=vmem,
        scratch_shapes=[
            half_words((chunks, members, capacity, LANES)),
            pltpu.VMEM((members, 8, capacity), jnp.int32),
            half_words((tok_dev, 2 * local_dim)),
            half_words((chunks, members, capacity, LANES)),
            pltpu.VMEM((members, 8, capacity), jnp.int32),
            half_words((tok_dev, members * capacity)),
            half_words((chunks, tok_dev, LANES)),
            half_words((chunks, halo_len, LANES)),
            half_words((chunks, halo_len, LANES)),
            words((band_rows + 2 * HALO, GRID_W + 2 * PAD, LANES)),
            half_words(weights.shape),
            half_words((chunks, LANES // head_dim, tok_dev, LANES)),
            half_words((chunks, LANES, tok_dev)),
            half_words((chunks, tok_dev, LANES)),
            half_words((chunks, LANES, tok_dev)),
            half_words((chunks, tok_dev, LANES)),
            words((chunks, tok_dev, LANES)),
            words((chunks, tok_dev, LANES)),
            words((chunks, tok_dev, LANES)),
            dma,
            dma((chunks, members)),
            dma((chunks, members)),
            dma((members,)),
            dma((members,)),
        ]
        + [dma((chunks,))] * 10,
        compiler_params=pltpu.CompilerParams(
            collective_id=0, has_side_effects=True, vmem_limit_bytes=VMEM_BYTES
        ),
        name="band",
    )(cells.reshape(1, tok_dev), features, weights, taps, bias)


def solution(mesh):
    placed = (
        P("seq", "head"),
        P("seq"),
        P(None, None, "head"),
        P(None, None, "head"),
        P(None, None, "head"),
        P("head"),
        P(None, None, "head"),
    )
    return jax.shard_map(
        shards, mesh=mesh, in_specs=placed, out_specs=P("seq", "head"), check_vma=False
    )
```

time: 155 us -> 118 us (0.76)
  Pallas kernels: 142 us -> 108 us
  other arithmetic: 3.48 us -> 0.68 us
    pallas_call x3 -> x1, Pallas kernels: 142 us -> 108 us  [shards(): pl.pallas_call(functools.partial(band_kernel, members, head_dim), out_sha...]
    unnamed x2 -> x12, local copies, waits for them, and re-layouts: 5.45 us -> 5.47 us
where the time goes in v2:
time: 118 us
  Pallas kernels  108 us (92%)
  local copies, waits for them, and re-layouts  9.08 us (8%)
    pallas_call x1, Pallas kernels, shards(): pl.pallas_call(functools.partial(band_kernel, members, head_dim), out_sha...  108 us
    unnamed x12, local copies, waits for them, and re-layouts  5.47 us
    reshape x1, local copies, waits for them, and re-layouts, shards(): weights = w_qkv.reshape(w_qkv.shape[0], 3 * local_dim)  2.95 us

profile of v2, /device:TPU:0, one launch (start us, length us, event | category | flops | bytes accessed | tf_op | source)
XLA Modules:
  0.0 117.9 jit_solution(15298671720721486951)
XLA Ops:
  0.0 3.2 %copy.9 = bf16[1024,3,512]{0,2,1:T(8,128)(2,1)S(1)} copy(bf16[1024,3,512]{2,0,1:T(8,128)(2,1)} %param.13) | data formatting | bytes 6291456 | tf_op args[6]
  3.2 0.0 copy-start
  3.2 0.0 copy-start.1
  3.2 0.0 copy-start.2
  3.2 0.0 copy-start.3
  3.2 0.0 copy-start.4
  3.2 3.0 %copy.10.weights_hbm = bf16[1024,1536]{1,0:T(8,128)(2,1)} copy(bf16[1024,1536]{0,1:T(8,128)(2,1)S(1)} %bitcast.3) | data formatting | bytes 6291456 | tf_op jit(solution)/shard_map/reshape | solution.py:474
  6.2 0.0 copy-done
  6.2 0.0 copy-done.1
  6.2 0.0 copy-done.2
  6.2 0.0 copy-done.3
  6.2 0.1 add_add_fusion
  6.3 0.7 reshape.17.taps_ref
  7.0 0.0 copy-done.4
  7.0 0.6 reshape.20
  7.6 108.1 %band.1 = bf16[1024,512]{1,0:T(8,128)(2,1)} custom-call(s32[1,1024]{1,0:T(1,128)} %bitcast.5, bf16[1024,512]{1,0:T(8,128)(2,1)} %features_ref.1, bf16[1024,1536]{1,0:T(8,128)(2,1)} %copy.10.weights_hbm, f32[49,512]{1,0:T(8,128)} %reshape.17.taps_ref, f32[1,512]{1,0:T(1,128)} %bitcast.4), custom_call_target="tpu_custom_call" | custom-call | tf_op jit(solution)/shard_map/band/pallas_call | solution.py:477
  115.6 2.3 %copy.12 = bf16[1024,512]{1,0:T(8,128)(2,1)} copy(bf16[1024,512]{1,0:T(8,128)(2,1)} %band.1) | data formatting | bytes 2097152
Async XLA Ops:
  3.2 3.0 %copy-start = (bf16[7,7,512]{2,1,0:T(8,128)(2,1)S(1)}, bf16[7,7,512]{2,1,0:T(8,128)(2,1)}, u32[]{:S(2)}) copy-start(bf16[7,7,512]{2,1,0:T(8,128)(2,1)} %param.9) | copy-start | bytes 150532
  3.2 3.0 %copy-start.1 = (bf16[5,5,512]{2,1,0:T(8,128)(2,1)S(1)}, bf16[5,5,512]{2,1,0:T(8,128)(2,1)}, u32[]{:S(2)}) copy-start(bf16[5,5,512]{2,1,0:T(8,128)(2,1)} %param.10) | copy-start | bytes 76804
  3.2 3.0 %copy-start.2 = (bf16[3,3,512]{2,1,0:T(4,128)(2,1)S(1)}, bf16[3,3,512]{2,1,0:T(4,128)(2,1)}, u32[]{:S(2)}) copy-start(bf16[3,3,512]{2,1,0:T(4,128)(2,1)} %param.11) | copy-start | bytes 27652
  3.2 3.0 %copy-start.3 = (f32[7,7]{1,0:T(8,128)S(1)}, f32[7,7]{1,0:T(8,128)}, u32[]{:S(2)}) copy-start(f32[7,7]{1,0:T(8,128)} %constant.7.clone.1) | copy-start | bytes 592
  3.2 3.7 %copy-start.4 = (bf16[512]{0:T(512)(128)(2,1)S(1)}, bf16[512]{0:T(512)(128)(2,1)}, u32[]{:S(2)}) copy-start(bf16[512]{0:T(512)(128)(2,1)} %param.12) | copy-start | bytes 3076

commit v3 on v2

--- a/solution.py
+++ b/solution.py
@@ -74,8 +74,12 @@
     value_recv,
 ):
     chunks, _, capacity, _ = outgoing_ref.shape
-    fetch = pltpu.make_async_copy(weights_hbm, weights_ref, weight_sem)
-    fetch.start()
+    fetches = [
+        pltpu.make_async_copy(weights_hbm.at[kind], weights_ref.at[kind], weight_sem.at[kind])
+        for kind in range(3)
+    ]
+    for fetch in fetches:
+        fetch.start()
     tok_dev, local_dim = out_ref.shape
     band_rows = tok_dev // GRID_W
     halo_len = HALO * GRID_W
@@ -301,7 +305,8 @@
         if chunk > 0:
             convolve(chunk - 1)
 
-    fetch.wait()
+    for fetch in fetches:
+        fetch.wait()
     for chunk in range(chunks):
         pair_copy(chunk).wait_recv()
 
@@ -332,15 +337,14 @@
 
     def project_keys(index, carry):
         rows = block_of(index)
-        product = jnp.dot(
-            mixed_ref[rows, :], weights_ref[:, local_dim:], preferred_element_type=jnp.float32
+        key_rows, value_rows = (
+            jnp.dot(mixed_ref[rows, :], weights_ref[kind], preferred_element_type=jnp.float32)
+            for kind in (1, 2)
         )
         for chunk in range(chunks):
-            first = chunk * LANES
-            keys = jnp.transpose(product[:, first : first + LANES])
-            keys_own[chunk, :, rows] = keys.astype(jnp.bfloat16)
-            first = local_dim + first
-            values_own[chunk, rows, :] = product[:, first : first + LANES].astype(jnp.bfloat16)
+            columns = slice(chunk * LANES, (chunk + 1) * LANES)
+            keys_own[chunk, :, rows] = jnp.transpose(key_rows[:, columns]).astype(jnp.bfloat16)
+            values_own[chunk, rows, :] = value_rows[:, columns].astype(jnp.bfloat16)
         return carry
 
     lax.fori_loop(0, blocks, project_keys, 0)
@@ -356,7 +360,7 @@
     def project_queries(index, carry):
         rows = block_of(index)
         product = jnp.dot(
-            mixed_ref[rows, :], weights_ref[:, :local_dim], preferred_element_type=jnp.float32
+            mixed_ref[rows, :], weights_ref[0], preferred_element_type=jnp.float32
         ).astype(jnp.bfloat16)
         for chunk in range(chunks):
             query = product[:, chunk * LANES : (chunk + 1) * LANES].astype(jnp.float32) * log_scale
@@ -471,7 +475,7 @@
     taps = merged.reshape(REACH * REACH, local_dim)
     bias = conv_bias.astype(jnp.float32).reshape(1, local_dim)
 
-    weights = w_qkv.reshape(w_qkv.shape[0], 3 * local_dim)
+    weights = jnp.transpose(w_qkv, (1, 0, 2))
     half_words = functools.partial(pltpu.VMEM, dtype=jnp.bfloat16)
     words = functools.partial(pltpu.VMEM, dtype=jnp.float32)
     return pl.pallas_call(
@@ -490,7 +494,7 @@
             half_words((chunks, halo_len, LANES)),
             half_words((chunks, halo_len, LANES)),
             words((band_rows + 2 * HALO, GRID_W + 2 * PAD, LANES)),
-            half_words(weights.shape),
+            half_words((3, 2 * local_dim, local_dim)),
             half_words((chunks, LANES // head_dim, tok_dev, LANES)),
             half_words((chunks, LANES, tok_dev)),
             half_words((chunks, tok_dev, LANES)),
@@ -499,7 +503,7 @@
             words((chunks, tok_dev, LANES)),
             words((chunks, tok_dev, LANES)),
             words((chunks, tok_dev, LANES)),
-            dma,
+            dma((3,)),
             dma((chunks, members)),
             dma((chunks, members)),
             dma((members,)),

time: 118 us -> 114 us (0.966)
  local copies, waits for them, and re-layouts: 9.08 us -> 2.92 us
  other arithmetic: 0.68 us -> 2.18 us
    unnamed x12 -> x1, local copies, waits for them, and re-layouts: 5.47 us -> 2.26 us
    reshape x1 -> x0, local copies, waits for them, and re-layouts: 2.95 us -> none  [shards(): weights = w_qkv.reshape(w_qkv.shape[0], 3 * local_dim)]
where the time goes in v3:
time: 114 us; the launch traced here: 113 us
  Pallas kernels  108 us (95%)
  local copies, waits for them, and re-layouts  2.92 us (3%)
  other arithmetic  2.18 us (2%)
    pallas_call x1, Pallas kernels, shards(): pl.pallas_call(functools.partial(band_kernel, members, head_dim), out_sha...  108 us

profile of v3, /device:TPU:0, one launch (start us, length us, event | category | flops | bytes accessed | tf_op | source)
XLA Modules:
  0.0 113.2 jit_solution(6451227296665462926)
XLA Ops:
  0.0 1.3 %reshape.16 = f32[512]{0:T(512)} convert(bf16[512]{0:T(512)(128)(2,1)} %param.12) | non-fusion elementwise | flops 512 | bytes 3072 | tf_op jit(solution)/shard_map/reshape | solution.py:476
  1.3 0.9 add_add_fusion
  2.2 0.7 reshape.13.taps_ref
  2.9 108.1 %band.1 = bf16[1024,512]{1,0:T(8,128)(2,1)} custom-call(s32[1,1024]{1,0:T(1,128)} %bitcast.5, bf16[1024,512]{1,0:T(8,128)(2,1)} %features_ref.1, bf16[3,1024,512]{2,1,0:T(8,128)(2,1)} %bitcast.3, f32[49,512]{1,0:T(8,128)} %reshape.13.taps_ref, f32[1,512]{1,0:T(1,128)} %bitcast.4), custom_call_target="tpu_custom_call" | custom-call | tf_op jit(solution)/shard_map/band/pallas_call | solution.py:481
  110.9 2.3 %copy.9 = bf16[1024,512]{1,0:T(8,128)(2,1)} copy(bf16[1024,512]{1,0:T(8,128)(2,1)} %band.1) | data formatting | bytes 2097152
